TPU v7x, 512 devices: a whole 4x4x16 slice. The times are simulated.
512 devices in a mesh: seq: 64 (over z, x), head: 2 (over core), dp: 4 (over y).
Axes of the slice: x: 4, y: 4, z: 16, core: 2. Of those that a mesh axis runs over, the one named last changes fastest.
Arguments:
- hidden: bfloat16 [4, 12288, 1024], P('dp', 'seq'), may hold values from -6 to 6
- norm_gain: float32 [1024], replicated, may hold values from 0.5 to 1.5
- projection: bfloat16 [3, 1024, 1024], P(None, None, 'head'), may hold values from -1 to 1
- upstream: bfloat16 [4, 12288, 1024], P('dp', 'seq', 'head'), may hold values from -6 to 6
- cluster: int32 [4, 12288, 1], P('dp', 'seq'), may hold values from 0 to 63; in each aligned block of 192 rows (0 to 191, 192 to 383, ..., all dimensions but the last counted through in order) at most 9 rows name the same one
Outputs:
- input_gradient: bfloat16 [4, 12288, 1024], P('dp', 'seq', 'head')
- gain_gradient: float32 [1024], P('head')
Inputs may be any that keep to these rules, and one draw needn't show every extreme that they name: Among the 192 tokens of one device no cluster is named more than 9 times, a bound that some block reaches.
All inputs are finite; a program needn't handle non-finite values.
Results may differ from a plain program's by a relative error of at most 0.01.
The roundings to bfloat16 on the way count: a program that leaves them out, or rounds other values in their place, can miss the bound.
Values may be sent and summed in bfloat16 or wider, within the bound.
No kernel may reach another device: no remote copies, remote signals or barrier semaphores. Data moves between devices by JAX's collectives and lax.ppermute only.
A program may use at most 64 MiB of HBM per device.

v0:
```python
import jax
import jax.numpy as jnp
from jax import lax
from jax.sharding import PartitionSpec as P

HDIM = 64
CLUS_DEV = 1
epsilon = 1e-05
masked = -1e30


def normalize(values, norm_gain):
    values = values.astype(jnp.float32)
    center = values - jnp.mean(values, -1, keepdims=True)
    spread = lax.rsqrt(jnp.mean(center * center, -1, keepdims=True) + epsilon)
    scaled = center * spread
    return (scaled, spread, (scaled * norm_gain).astype(jnp.bfloat16))


def attend_backward(queries, key_rows, values, upstream, allowed, factor):
    scores = (
        lax.dot_general(
            queries, key_rows, (((1,), (1,)), ((), ())), preferred_element_type=jnp.float32
        )
        * factor
    )
    scores = jnp.where(allowed, scores, masked)
    powers = jnp.exp(scores - jnp.max(scores, -1, keepdims=True))
    weights = powers / jnp.sum(powers, -1, keepdims=True)
    rounded = weights.astype(jnp.bfloat16)
    output = jnp.dot(rounded, values, preferred_element_type=jnp.float32)
    center_term = jnp.sum(upstream.astype(jnp.float32) * output, -1, keepdims=True)
    grad_values = lax.dot_general(
        rounded, upstream, (((0,), (0,)), ((), ())), preferred_element_type=jnp.float32
    ).astype(jnp.bfloat16)
    grad_weights = lax.dot_general(
        upstream, values, (((1,), (1,)), ((), ())), preferred_element_type=jnp.float32
    )
    grad_scores = (weights * (grad_weights - center_term) * factor).astype(jnp.bfloat16)
    grad_queries = jnp.dot(grad_scores, key_rows, preferred_element_type=jnp.float32).astype(
        jnp.bfloat16
    )
    grad_keys = lax.dot_general(
        grad_scores, queries, (((0,), (0,)), ((), ())), preferred_element_type=jnp.float32
    ).astype(jnp.bfloat16)
    return (grad_queries, grad_keys, grad_values)


def cluster_grads(payload, validity, head_width):
    row_count = payload.shape[0]
    spans = payload.shape[1] // 4
    heads_local = spans // head_width
    positions = lax.broadcasted_iota(jnp.int32, (row_count, row_count), 0)
    others = lax.broadcasted_iota(jnp.int32, (row_count, row_count), 1)
    allowed = (positions >= others) & (validity[None, :] > 0)
    factor = head_width ** (-0.5)

    def one_head(head_index, result):
        offset = head_index * head_width

        def select(portion):
            return lax.dynamic_slice_in_dim(payload, portion * spans + offset, head_width, 1)

        grads_head = attend_backward(select(0), select(1), select(2), select(3), allowed, factor)
        for portion in range(3):
            result = lax.dynamic_update_slice_in_dim(
                result, grads_head[portion], portion * spans + offset, 1
            )
        return result

    return lax.fori_loop(0, heads_local, one_head, jnp.zeros((row_count, 3 * spans), jnp.bfloat16))


def on_device(hidden, norm_gain, projection, upstream, cluster):
    seq_count = lax.axis_size("seq")
    tokens = hidden.shape[1]
    width_model = hidden.shape[2]
    spans = projection.shape[2]
    clusters_all = CLUS_DEV * seq_count
    slot_rows = 3 * tokens // clusters_all
    scaled, spread, normed = normalize(hidden[0], norm_gain)
    labels = cluster[0, :, 0]
    member = (labels[:, None] == jnp.arange(clusters_all, dtype=jnp.int32)[None, :]).astype(
        jnp.int32
    )
    ranks = jnp.sum(jnp.cumsum(member, 0) * member, 1) - 1
    target = labels * slot_rows + ranks
    projected = jnp.einsum(
        "td,kdh->tkh", normed, projection, preferred_element_type=jnp.float32
    ).astype(jnp.bfloat16)
    payload = jnp.concatenate([projected.reshape(tokens, 3 * spans), upstream[0]], 1)
    columns = payload.shape[1]
    outgoing = jnp.zeros((clusters_all * slot_rows, columns), jnp.bfloat16).at[target].set(payload)
    outgoing = outgoing.reshape(seq_count, CLUS_DEV, slot_rows, columns)
    present = jnp.zeros((clusters_all * slot_rows,), jnp.bfloat16).at[target].set(1.0)
    present = present.reshape(seq_count, CLUS_DEV, slot_rows)
    rows_in = lax.all_to_all(outgoing, "seq", split_axis=0, concat_axis=0, tiled=True)
    marks_in = lax.all_to_all(present, "seq", split_axis=0, concat_axis=0, tiled=True)
    sources = rows_in.shape[0]
    item_count = rows_in.shape[1]
    stacked = jnp.swapaxes(rows_in, 0, 1).reshape(item_count, sources * slot_rows, rows_in.shape[3])
    mark_rows = jnp.swapaxes(marks_in, 0, 1).reshape(item_count, sources * slot_rows)

    def per_item(entries):
        return cluster_grads(entries[0], entries[1].astype(jnp.float32), HDIM)

    results = lax.map(per_item, (stacked, mark_rows))
    width_out = results.shape[-1]
    results = results.reshape(item_count, sources, slot_rows, width_out)
    answer = jnp.swapaxes(results, 0, 1)
    returned = lax.all_to_all(answer, "seq", split_axis=0, concat_axis=0, tiled=True)
    restored = returned.reshape(clusters_all * slot_rows, 3 * spans)[target]
    partial_value = jnp.einsum(
        "tkh,kdh->td",
        restored.reshape(tokens, 3, spans),
        projection,
        preferred_element_type=jnp.float32,
    )
    partial_value = lax.optimization_barrier(partial_value.astype(jnp.bfloat16)).astype(jnp.float32)
    half_width = width_model // lax.axis_size("head")
    offset = lax.axis_index("head") * half_width
    own_scaled = lax.dynamic_slice_in_dim(scaled, offset, half_width, 1)
    own_gain = lax.dynamic_slice_in_dim(norm_gain, offset, half_width, 0)
    gradient = lax.psum_scatter(
        partial_value.astype(jnp.bfloat16), "head", scatter_dimension=1, tiled=True
    ).astype(jnp.float32)
    scaled_grad = gradient * own_gain
    first_sum, second_sum = lax.psum(
        (
            jnp.sum(scaled_grad, -1, keepdims=True),
            jnp.sum(scaled_grad * own_scaled, -1, keepdims=True),
        ),
        "head",
    )
    first_mean = first_sum / width_model
    second_mean = second_sum / width_model
    input_gradient = (spread * (scaled_grad - first_mean - own_scaled * second_mean)).astype(
        jnp.bfloat16
    )
    local_sum = jnp.sum(gradient * own_scaled, 0)
    gain_total = lax.psum(local_sum, ("seq", "dp"))
    gain_gradient = gain_total * (seq_count * lax.axis_size("dp") * tokens) ** (-0.5)
    return (input_gradient.reshape(1, tokens, half_width), gain_gradient)


def solution(mesh):
    in_specs = (
        P("dp", "seq", None),
        P(),
        P(None, None, "head"),
        P("dp", "seq", "head"),
        P("dp", "seq", None),
    )
    out_specs = (P("dp", "seq", "head"), P("head"))
    return jax.shard_map(
        on_device, mesh=mesh, in_specs=in_specs, out_specs=out_specs, check_vma=False
    )
```

profile of v0, /device:TPU:1, one launch (start us, length us, event | category | flops | bytes accessed | tf_op | source)
XLA Modules:
  0.0 1259.5 jit_solution(10916248163489631353)
XLA Ops:
  12.9 19.1 %all-to-all-start.1 = ((bf16[64,1,9]{2,1,0:T(2,128)(2,1)}), bf16[64,1,9]{2,1,0:T(2,128)(2,1)S(1)}, u32[]{:S(2)}, u32[]{:S(2)}) async-start(bf16[64,1,9]{2,1,0:T(2,128)(2,1)} %reshape.133), calls=%async_computation.1 | async-start | bytes 65536 | tf_op jit(solution)/shard_map/all_to_all | solution.py:98
  37.2 4.1 scatter_custom_fusion
  41.3 4.6 reshape.101
  45.9 14.8 %all-to-all-start = ((bf16[64,1,9,2048]{3,2,1,0:T(8,128)(2,1)}), bf16[64,1,9,2048]{3,2,1,0:T(8,128)(2,1)}, u32[]{:S(2)}, u32[]{:S(2)}) async-start(bf16[64,1,9,2048]{3,2,1,0:T(8,128)(2,1)} %bitcast.69), calls=%async_computation | async-start | bytes 8388608 | tf_op jit(solution)/shard_map/all_to_all | solution.py:97
  61.0 183.4 %all-to-all-done = bf16[64,1,9,2048]{3,2,1,0:T(8,128)(2,1)} async-done(((bf16[64,1,9,2048]{3,2,1,0:T(8,128)(2,1)}), bf16[64,1,9,2048]{3,2,1,0:T(8,128)(2,1)}, u32[]{:S(2)}, u32[]{:S(2)}) %all-to-all-start) | async-done | bytes 2359328 | tf_op jit(solution)/shard_map/all_to_all | solution.py:97
  244.3 4.7 squeeze.14
  249.0 4.3 copy.24
  254.8 113.3 %while.24 = (s32[]{:T(128)}, bf16[576,1536]{0,1:T(8,128)(2,1)}, bf16[576,2048]{0,1:T(8,128)(2,1)}, pred[576]{0:T(1024)(128)(4,1)S(1)}, s32[]{:T(128)}, /*index=5...) while((s32[]{:T(128)}, bf16[576,1536]{0,1:T(8,128)(2,1)}, ...), condition=%wide.region_11.12_spmd.clone, body=%wide.region_7.11_spmd.clone.sunk | while | flops 260331856 | bytes 16045296 | solution.py:71
  259.8 2.9 multiply_convert_fusion.3
  262.7 2.1 fusion.91
  264.7 2.1 fusion.92
  266.8 2.1 fusion.93
  274.0 2.9 multiply_convert_fusion.3
  276.9 2.0 fusion.91
  278.9 2.1 fusion.92
  281.0 2.1 fusion.93
  288.2 2.9 multiply_convert_fusion.3
  291.0 2.1 fusion.91
  293.1 2.1 fusion.92
  295.2 2.1 fusion.93
  302.3 2.9 multiply_convert_fusion.3
  307.3 2.1 fusion.92
  309.4 2.1 fusion.93
  316.5 2.9 multiply_convert_fusion.3
  321.4 2.1 fusion.92
  323.5 2.1 fusion.93
  330.7 2.9 multiply_convert_fusion.3
  333.5 2.1 fusion.91
  335.6 2.1 fusion.92
  337.7 2.1 fusion.93
  344.8 2.9 multiply_convert_fusion.3
  347.7 2.1 fusion.91
  349.7 2.1 fusion.92
  351.8 2.1 fusion.93
  359.0 2.9 multiply_convert_fusion.3
  361.8 2.1 fusion.91
  363.9 2.1 fusion.92
  366.0 2.1 fusion.93
  368.1 3.9 copy.25
  372.0 4.2 transpose_reshape.3
  376.2 11.6 all-to-all-start.2
  388.1 137.9 %all-to-all-done.2 = bf16[64,1,9,1536]{3,2,1,0:T(8,128)(2,1)} async-done(((bf16[64,1,9,1536]{3,2,1,0:T(8,128)(2,1)}), bf16[64,1,9,1536]{3,2,1,0:T(8,128)(2,1)}, u32[]{:S(2)}, u32[]{:S(2)}) %all-to-all-start.2) | async-done | bytes 1769504 | tf_op jit(solution)/shard_map/all_to_all | solution.py:111
  526.0 4.2 reshape.103
  530.2 4.1 gather_fusion
  534.4 3.0 fusion.24
  538.6 17.6 %reduce-scatter.2.cloned.1.call-done = bf16[192,512]{1,0:T(8,128)(2,1)} async-done(((bf16[192,1024]{1,0:T(8,128)(2,1)}), bf16[192,512]{1,0:T(8,128)(2,1)}) %reduce-scatter.2.cloned.1.call-update) | async-done | bytes 196624 | tf_op jit(solution)/shard_map/reduce_scatter | solution.py:124
  557.6 579.8 %psum.23 = f32[512]{0:T(512)S(1)} all-reduce(f32[512]{0:T(512)S(1)} %get-tuple-element.173), channel_id=1, replica_groups=mesh['seq'=64,'head'=2,'dp'=4] {'seq','dp'}, use_global_device_ids=true, to_apply=%region_18.19 | all-reduce | flops 512 | bytes 4096 | tf_op jit(solution)/shard_map/psum | solution.py:141
  1138.0 112.8 %all-reduce.1 = (f32[192,1]{0,1:T(1,128)S(1)}, f32[192,1]{0,1:T(1,128)S(1)}) all-reduce(f32[192,1]{0,1:T(1,128)S(1)} %bitcast.76, f32[192,1]{0,1:T(1,128)S(1)} %bitcast.77), channel_id=1, replica_groups=mesh['seq'=64,'head'=2,'dp'=4] {'head'}, use_global_device_ids=true, to_apply=%region_16.17 | all-reduce | flops 384 | bytes 3072 | tf_op jit(solution)/shard_map/psum | solution.py:128
  (90 shorter events, 62.1 us)
Async XLA Ops:
  7.2 27.3 %copy-start = (bf16[3,1024,512]{2,1,0:T(8,128)(2,1)S(1)}, bf16[3,1024,512]{2,1,0:T(8,128)(2,1)}, u32[]{:S(2)}) copy-start(bf16[3,1024,512]{2,1,0:T(8,128)(2,1)} %param.9) | copy-start | bytes 9437188
  12.9 33.0 %all-to-all-start.1 = ((bf16[64,1,9]{2,1,0:T(2,128)(2,1)}), bf16[64,1,9]{2,1,0:T(2,128)(2,1)S(1)}, u32[]{:S(2)}, u32[]{:S(2)}) async-start(bf16[64,1,9]{2,1,0:T(2,128)(2,1)} %reshape.133), calls=%async_computation.1 | async-start | bytes 65536 | tf_op jit(solution)/shard_map/all_to_all | solution.py:98
  34.4 2.8 copy-start.3
  45.9 198.5 %all-to-all-start = ((bf16[64,1,9,2048]{3,2,1,0:T(8,128)(2,1)}), bf16[64,1,9,2048]{3,2,1,0:T(8,128)(2,1)}, u32[]{:S(2)}, u32[]{:S(2)}) async-start(bf16[64,1,9,2048]{3,2,1,0:T(8,128)(2,1)} %bitcast.69), calls=%async_computation | async-start | bytes 8388608 | tf_op jit(solution)/shard_map/all_to_all | solution.py:97
  256.1 1.2 copy-start.1
  270.3 1.2 copy-start.1
  284.5 1.2 copy-start.1
  298.7 1.2 copy-start.1
  312.8 1.2 copy-start.1
  327.0 1.2 copy-start.1
  341.1 1.2 copy-start.1
  355.3 1.2 copy-start.1
  376.2 149.7 %all-to-all-start.2 = ((bf16[64,1,9,1536]{3,2,1,0:T(8,128)(2,1)}), bf16[64,1,9,1536]{3,2,1,0:T(8,128)(2,1)}, u32[]{:S(2)}, u32[]{:S(2)}) async-start(bf16[64,1,9,1536]{3,2,1,0:T(8,128)(2,1)} %bitcast.70), calls=%async_computation.2 | async-start | bytes 6291456 | tf_op jit(solution)/shard_map/all_to_all | solution.py:111
  387.8 168.4 %reduce-scatter.2.cloned.1.call-start = ((), (), s32[]{:S(2)}) async-start(), calls=%async_computation.4 | async-start | bytes 589824 | tf_op jit(solution)/shard_map/reduce_scatter | solution.py:124
  534.4 3.1 copy-start.4
  534.4 3.1 copy-start.2
Sparse Core Ops, SparseCore 0:
  537.5 18.6 reduce-scatter.1
where the time goes:
time: 1260 us
  blocking collectives  693 us (55%)
  waiting for transfers between devices  339 us (27%)
  matrix products  99.9 us (8%)
  starting transfers between devices  45.7 us (4%)
  local copies, waits for them, and re-layouts  42.7 us (3%)
  other arithmetic  25.4 us (2%)
  between operations  14.2 us (1%)
    psum x1, blocking collectives, on_device(): gain_total = lax.psum(local_sum, ('seq', 'dp'))  580 us
    all_to_all x1, waiting for transfers between devices, on_device(): lax.all_to_all(outgoing, 'seq', split_axis=0, concat_axis=0, tiled=True)  183 us
    all_to_all x1, waiting for transfers between devices, on_device(): lax.all_to_all(answer, 'seq', split_axis=0, concat_axis=0, tiled=True)  138 us
    psum x1, blocking collectives, on_device(): lax.psum((jnp.sum(scaled_grad, -1, keepdims=True), jnp.sum(scaled_grad *...  113 us
  transfers between devices with their start and end apart: 4, of which 3 were waited for; matrix products, arithmetic and copies ran while one was open for 1% of the time, Pallas kernels for 0%

commit v1 on v0

--- a/solution.py
+++ b/solution.py
@@ -138,7 +138,7 @@
         jnp.bfloat16
     )
     local_sum = jnp.sum(gradient * own_scaled, 0)
-    gain_total = lax.psum(local_sum, ("seq", "dp"))
+    gain_total = jnp.sum(lax.all_gather(local_sum, ("seq", "dp")), axis=0)
     gain_gradient = gain_total * (seq_count * lax.axis_size("dp") * tokens) ** (-0.5)
     return (input_gradient.reshape(1, tokens, half_width), gain_gradient)
 

time: 1260 us -> 1300 us (1.032)
  blocking collectives: 693 us -> 727 us
    all_gather x0 -> x1, blocking collectives: none -> 615 us  [on_device(): gain_total = jnp.sum(lax.all_gather(local_sum, ('seq', 'dp')), axis=0)]
    psum x1 -> x0, blocking collectives: 580 us -> none  [on_device(): gain_total = lax.psum(local_sum, ('seq', 'dp'))]
where the time goes in v1:
time: 1300 us
  blocking collectives  727 us (56%)
  waiting for transfers between devices  339 us (26%)
  matrix products  99.9 us (8%)
  starting transfers between devices  45.7 us (4%)
  local copies, waits for them, and re-layouts  42.7 us (3%)
  other arithmetic  26.8 us (2%)
  between operations  14.2 us (1%)
    all_gather x1, blocking collectives, on_device(): gain_total = jnp.sum(lax.all_gather(local_sum, ('seq', 'dp')), axis=0)  615 us
    all_to_all x1, waiting for transfers between devices, on_device(): lax.all_to_all(outgoing, 'seq', split_axis=0, concat_axis=0, tiled=True)  183 us
    all_to_all x1, waiting for transfers between devices, on_device(): lax.all_to_all(answer, 'seq', split_axis=0, concat_axis=0, tiled=True)  138 us
    psum x1, blocking collectives, on_device(): lax.psum((jnp.sum(scaled_grad, -1, keepdims=True), jnp.sum(scaled_grad *...  113 us
  transfers between devices with their start and end apart: 4, of which 3 were waited for; matrix products, arithmetic and copies ran while one was open for 1% of the time, Pallas kernels for 0%

profile of v1, /device:TPU:1, one launch (start us, length us, event | category | flops | bytes accessed | tf_op | source)
XLA Modules:
  0.0 1295.6 jit_solution(17263034300938739672)
XLA Ops:
  12.9 19.1 %all-to-all-start.1 = ((bf16[64,1,9]{2,1,0:T(2,128)(2,1)}), bf16[64,1,9]{2,1,0:T(2,128)(2,1)S(1)}, u32[]{:S(2)}, u32[]{:S(2)}) async-start(bf16[64,1,9]{2,1,0:T(2,128)(2,1)} %reshape.137), calls=%async_computation.1 | async-start | bytes 65536 | tf_op jit(solution)/shard_map/all_to_all | solution.py:98
  37.2 4.1 scatter_custom_fusion
  41.3 4.6 reshape.101
  45.9 14.8 %all-to-all-start = ((bf16[64,1,9,2048]{3,2,1,0:T(8,128)(2,1)}), bf16[64,1,9,2048]{3,2,1,0:T(8,128)(2,1)}, u32[]{:S(2)}, u32[]{:S(2)}) async-start(bf16[64,1,9,2048]{3,2,1,0:T(8,128)(2,1)} %bitcast.70), calls=%async_computation | async-start | bytes 8388608 | tf_op jit(solution)/shard_map/all_to_all | solution.py:97
  61.0 183.4 %all-to-all-done = bf16[64,1,9,2048]{3,2,1,0:T(8,128)(2,1)} async-done(((bf16[64,1,9,2048]{3,2,1,0:T(8,128)(2,1)}), bf16[64,1,9,2048]{3,2,1,0:T(8,128)(2,1)}, u32[]{:S(2)}, u32[]{:S(2)}) %all-to-all-start) | async-done | bytes 2359328 | tf_op jit(solution)/shard_map/all_to_all | solution.py:97
  244.3 4.7 squeeze.14
  249.0 4.3 copy.24
  254.8 113.3 %while.24 = (s32[]{:T(128)}, bf16[576,1536]{0,1:T(8,128)(2,1)}, bf16[576,2048]{0,1:T(8,128)(2,1)}, pred[576]{0:T(1024)(128)(4,1)S(1)}, s32[]{:T(128)}, /*index=5...) while((s32[]{:T(128)}, bf16[576,1536]{0,1:T(8,128)(2,1)}, ...), condition=%wide.region_11.12_spmd.clone, body=%wide.region_7.11_spmd.clone.sunk | while | flops 260331856 | bytes 16045296 | solution.py:71
  259.8 2.9 multiply_convert_fusion.3
  262.7 2.1 fusion.91
  264.7 2.1 fusion.92
  266.8 2.1 fusion.93
  274.0 2.9 multiply_convert_fusion.3
  276.9 2.0 fusion.91
  278.9 2.1 fusion.92
  281.0 2.1 fusion.93
  288.2 2.9 multiply_convert_fusion.3
  291.0 2.1 fusion.91
  293.1 2.1 fusion.92
  295.2 2.1 fusion.93
  302.3 2.9 multiply_convert_fusion.3
  307.3 2.1 fusion.92
  309.4 2.1 fusion.93
  316.5 2.9 multiply_convert_fusion.3
  321.4 2.1 fusion.92
  323.5 2.1 fusion.93
  330.7 2.9 multiply_convert_fusion.3
  333.5 2.1 fusion.91
  335.6 2.1 fusion.92
  337.7 2.1 fusion.93
  344.8 2.9 multiply_convert_fusion.3
  347.7 2.1 fusion.91
  349.7 2.1 fusion.92
  351.8 2.1 fusion.93
  359.0 2.9 multiply_convert_fusion.3
  361.8 2.1 fusion.91
  363.9 2.1 fusion.92
  366.0 2.1 fusion.93
  368.1 3.9 copy.25
  372.0 4.2 transpose_reshape.3
  376.2 11.6 all-to-all-start.2
  388.1 137.9 %all-to-all-done.2 = bf16[64,1,9,1536]{3,2,1,0:T(8,128)(2,1)} async-done(((bf16[64,1,9,1536]{3,2,1,0:T(8,128)(2,1)}), bf16[64,1,9,1536]{3,2,1,0:T(8,128)(2,1)}, u32[]{:S(2)}, u32[]{:S(2)}) %all-to-all-start.2) | async-done | bytes 1769504 | tf_op jit(solution)/shard_map/all_to_all | solution.py:111
  526.0 4.2 reshape.103
  530.2 4.1 gather_fusion
  534.4 3.0 fusion.24
  538.6 17.6 %reduce-scatter.2.cloned.1.call-done = bf16[192,512]{1,0:T(8,128)(2,1)} async-done(((bf16[192,1024]{1,0:T(8,128)(2,1)}), bf16[192,512]{1,0:T(8,128)(2,1)}) %reduce-scatter.2.cloned.1.call-update) | async-done | bytes 196624 | tf_op jit(solution)/shard_map/reduce_scatter | solution.py:124
  557.6 614.6 %all-gather.1 = f32[256,1,512]{2,1,0:T(1,128)} all-gather(f32[1,1,512]{2,1,0:T(1,128)S(1)} %bitcast.77), channel_id=2, replica_groups=mesh['seq'=64,'head'=2,'dp'=4] {'seq','dp'}, dimensions={0}, use_global_device_ids=true | all-gather | bytes 526336 | tf_op jit(solution)/shard_map/all_gather | solution.py:141
  1174.1 112.7 %all-reduce.1 = (f32[192,1]{0,1:T(1,128)S(1)}, f32[192,1]{0,1:T(1,128)S(1)}) all-reduce(f32[192,1]{0,1:T(1,128)S(1)} %bitcast.78, f32[192,1]{0,1:T(1,128)S(1)} %bitcast.79), channel_id=1, replica_groups=mesh['seq'=64,'head'=2,'dp'=4] {'head'}, use_global_device_ids=true, to_apply=%region_16.17 | all-reduce | flops 384 | bytes 3072 | tf_op jit(solution)/shard_map/psum | solution.py:128
  (91 shorter events, 63.5 us)
Async XLA Ops:
  7.2 27.3 %copy-start = (bf16[3,1024,512]{2,1,0:T(8,128)(2,1)S(1)}, bf16[3,1024,512]{2,1,0:T(8,128)(2,1)}, u32[]{:S(2)}) copy-start(bf16[3,1024,512]{2,1,0:T(8,128)(2,1)} %param.9) | copy-start | bytes 9437188
  12.9 33.0 %all-to-all-start.1 = ((bf16[64,1,9]{2,1,0:T(2,128)(2,1)}), bf16[64,1,9]{2,1,0:T(2,128)(2,1)S(1)}, u32[]{:S(2)}, u32[]{:S(2)}) async-start(bf16[64,1,9]{2,1,0:T(2,128)(2,1)} %reshape.137), calls=%async_computation.1 | async-start | bytes 65536 | tf_op jit(solution)/shard_map/all_to_all | solution.py:98
  34.4 2.8 copy-start.3
  45.9 198.5 %all-to-all-start = ((bf16[64,1,9,2048]{3,2,1,0:T(8,128)(2,1)}), bf16[64,1,9,2048]{3,2,1,0:T(8,128)(2,1)}, u32[]{:S(2)}, u32[]{:S(2)}) async-start(bf16[64,1,9,2048]{3,2,1,0:T(8,128)(2,1)} %bitcast.70), calls=%async_computation | async-start | bytes 8388608 | tf_op jit(solution)/shard_map/all_to_all | solution.py:97
  256.1 1.2 copy-start.1
  270.3 1.2 copy-start.1
  284.5 1.2 copy-start.1
  298.7 1.2 copy-start.1
  312.8 1.2 copy-start.1
  327.0 1.2 copy-start.1
  341.1 1.2 copy-start.1
  355.3 1.2 copy-start.1
  376.2 149.7 %all-to-all-start.2 = ((bf16[64,1,9,1536]{3,2,1,0:T(8,128)(2,1)}), bf16[64,1,9,1536]{3,2,1,0:T(8,128)(2,1)}, u32[]{:S(2)}, u32[]{:S(2)}) async-start(bf16[64,1,9,1536]{3,2,1,0:T(8,128)(2,1)} %bitcast.71), calls=%async_computation.2 | async-start | bytes 6291456 | tf_op jit(solution)/shard_map/all_to_all | solution.py:111
  387.8 168.4 %reduce-scatter.2.cloned.1.call-start = ((), (), s32[]{:S(2)}) async-start(), calls=%async_computation.4 | async-start | bytes 589824 | tf_op jit(solution)/shard_map/reduce_scatter | solution.py:124
  534.4 3.1 copy-start.4
  534.4 3.1 copy-start.2
Sparse Core Ops, SparseCore 0:
  537.5 18.6 reduce-scatter.1
